TPU v7x, 128 devices: a whole 4x4x4 slice. The times are simulated.
128 devices in a mesh: dp: 8 (over y, z_lo), fsdp: 16 (over z_hi, x, core).
Axes of the slice: x: 4, y: 4, z: 4 (z_hi: 2, z_lo: 2; z = z_hi * 2 + z_lo), core: 2. Of those that a mesh axis runs over, the one named last changes fastest.
Arguments:
- acts: bfloat16 [4096, 8192], P('dp', 'fsdp'), may hold values from -6 to 6
- grads_out: bfloat16 [4096, 12288], P('dp', 'fsdp'), may hold values from -0.0625 to 0.0625
- basis: bfloat16 [8192, 512], P('fsdp'), may hold values from -0.375 to 0.375
- first_moment: float32 [512, 12288], P('fsdp', 'dp'), may hold values from -6 to 6
- second_moment: float32 [512, 12288], P('fsdp', 'dp'), may hold values from 0.002 to 0.02
Outputs:
- update: bfloat16 [8192, 12288], P('fsdp', 'dp')
- moment_one: float32 [512, 12288], P('fsdp', 'dp')
- moment_two: float32 [512, 12288], P('fsdp', 'dp')
All inputs are finite; a program needn't handle non-finite values.
Results may differ from a plain program's by a relative error of at most 0.0049.
Values may be sent and summed in bfloat16 or wider, within the bound.
A program may use at most 128 MiB of HBM per device.

v0:
```python
import jax
import jax.numpy as jnp
from jax import lax
from jax.sharding import PartitionSpec as P

bias_one = 1.0 - 0.9**10
bias_two = 1.0 - 0.999**10
adam_eps = 1e-08
galore_scale = 0.25


def shards(acts, grads_out, basis, first_moment, second_moment):
    basis_wide = basis.astype(jnp.float32)
    partial_value = lax.dot_general(
        basis_wide,
        lax.dot_general(
            acts,
            lax.all_gather(grads_out, "fsdp", axis=1, tiled=True),
            (((0,), (0,)), ((), ())),
            preferred_element_type=jnp.float32,
        ),
        (((0,), (0,)), ((), ())),
        precision=lax.Precision.HIGHEST,
    )
    rowwise = lax.psum_scatter(partial_value, "fsdp", scatter_dimension=0, tiled=True)
    shares = lax.psum_scatter(rowwise, "dp", scatter_dimension=1, tiled=True)
    moment_one = 0.9 * first_moment + 0.1 * shares
    moment_two = 0.999 * second_moment + 0.001 * shares * shares
    normed = (moment_one / bias_one / (jnp.sqrt(moment_two / bias_two) + adam_eps)).astype(
        jnp.bfloat16
    )
    full_rank = lax.all_gather(normed, "fsdp", axis=0, tiled=True)
    update = (galore_scale * jnp.dot(basis, full_rank, preferred_element_type=jnp.float32)).astype(
        jnp.bfloat16
    )
    return (update, moment_one, moment_two)


def solution(mesh):
    return jax.shard_map(
        shards,
        mesh=mesh,
        in_specs=(
            P("dp", "fsdp"),
            P("dp", "fsdp"),
            P("fsdp", None),
            P("fsdp", "dp"),
            P("fsdp", "dp"),
        ),
        out_specs=(P("fsdp", "dp"), P("fsdp", "dp"), P("fsdp", "dp")),
        check_vma=False,
    )
```

profile of v0, /device:TPU:1, one launch (start us, length us, event | category | flops | bytes accessed | tf_op | source)
XLA Modules:
  0.0 463.1 jit_solution(17052677865715637723)
XLA Ops:
  7.2 0.0 copy-start
  7.2 0.0 all-gather.3.cloned.1.call-start
  7.2 0.7 all-gather.3.cloned.1.call-update
  7.9 0.0 reduce-scatter.7.cloned.1.call-start
  8.0 96.3 %all-gather.3.cloned.1.call-done = bf16[512,12288]{1,0:T(8,128)(2,1)} async-done(((bf16[512,768]{1,0:T(8,128)(2,1)}), bf16[512,12288]{1,0:T(8,128)(2,1)}) %all-gather.3.cloned.1.call-update) | async-done | bytes 12582928 | tf_op jit(solution)/shard_map/all_gather | solution.py:18
  104.3 14.7 %fusion.4 = f32[512,12288]{1,0:T(8,128)} fusion(bf16[512,512]{1,0:T(8,128)(2,1)} %param.5, bf16[512,12288]{1,0:T(8,128)(2,1)} %all-gather.3.cloned.1.call-done), kind=kOutput, calls=%fused_computation.8 | convolution fusion | flops 6442450944 | bytes 38273024 | tf_op jit(solution)/shard_map/dot_general | solution.py:16
  119.0 0.0 copy-done
  119.0 26.8 %convolution_bitcast_fusion = f32[512,12288]{0,1:T(8,128)} fusion(f32[512,12288]{1,0:T(8,128)} %fusion.4, bf16[512,512]{1,0:T(8,128)(2,1)S(1)} %copy-done), kind=kOutput, calls=%fused_computation | convolution fusion | flops 38654705664 | bytes 50855936 | tf_op jit(solution)/shard_map/dot_general | solution.py:14
  145.7 24.7 %copy.21 = f32[512,12288]{1,0:T(8,128)} copy(f32[512,12288]{0,1:T(8,128)} %convolution_bitcast_fusion) | data formatting | bytes 50331648
  170.5 0.0 copy-start.1
  170.5 0.0 copy-start.2
  170.5 0.0 reduce-scatter.7.cloned.1.call-update
  170.5 0.0 reduce-scatter.5.cloned.1.call-start
  170.5 187.5 %reduce-scatter.7.cloned.1.call-done = f32[32,12288]{1,0:T(8,128)} async-done(((f32[512,12288]{1,0:T(8,128)}), f32[32,12288]{1,0:T(8,128)}) %reduce-scatter.7.cloned.1.call-update) | async-done | bytes 1572880 | tf_op jit(solution)/shard_map/reduce_scatter | solution.py:25
  358.0 0.0 reduce-scatter.5.cloned.1.call-update
  358.0 0.0 all-gather.5.cloned.1.call-start
  358.1 42.1 %reduce-scatter.5.cloned.1.call-done = f32[32,1536]{1,0:T(8,128)} async-done(((f32[32,12288]{1,0:T(8,128)}), f32[32,1536]{1,0:T(8,128)}) %reduce-scatter.5.cloned.1.call-update) | async-done | bytes 196624 | tf_op jit(solution)/shard_map/reduce_scatter | solution.py:26
  400.1 0.0 copy-done.1
  400.1 0.0 copy-done.2
  400.1 1.8 divide_convert_fusion
  401.9 0.0 all-gather.5.cloned.1.call-update
  401.9 50.6 %all-gather.5.cloned.1.call-done = bf16[512,1536]{1,0:T(8,128)(2,1)} async-done(((bf16[32,1536]{1,0:T(8,128)(2,1)}), bf16[512,1536]{1,0:T(8,128)(2,1)}) %all-gather.5.cloned.1.call-update) | async-done | bytes 1572880 | tf_op jit(solution)/shard_map/all_gather | solution.py:32
  452.6 2.4 fusion.1
  455.0 1.6 copy.20
Async XLA Ops:
  7.2 111.8 %copy-start = (bf16[512,512]{1,0:T(8,128)(2,1)S(1)}, bf16[512,512]{1,0:T(8,128)(2,1)}, u32[]{:S(2)}) copy-start(bf16[512,512]{1,0:T(8,128)(2,1)} %param.7) | copy-start | bytes 1572868
  7.2 97.1 %all-gather.3.cloned.1.call-start = ((), (), s32[]{:S(2)}) async-start(), calls=%async_computation.2 | async-start | bytes 13369344 | tf_op jit(solution)/shard_map/all_gather | solution.py:18
  7.9 350.1 %reduce-scatter.7.cloned.1.call-start = ((), (), s32[]{:S(2)}) async-start(), calls=%async_computation.5 | async-start | bytes 26738688 | tf_op jit(solution)/shard_map/reduce_scatter | solution.py:25
  170.5 229.7 %copy-start.1 = (f32[32,1536]{1,0:T(8,128)S(1)}, f32[32,1536]{1,0:T(8,128)}, u32[]{:S(2)}) copy-start(f32[32,1536]{1,0:T(8,128)} %param.8) | copy-start | bytes 589828
  170.5 229.7 %copy-start.2 = (f32[32,1536]{1,0:T(8,128)S(1)}, f32[32,1536]{1,0:T(8,128)}, u32[]{:S(2)}) copy-start(f32[32,1536]{1,0:T(8,128)} %param.9) | copy-start | bytes 589828
  170.5 229.6 %reduce-scatter.5.cloned.1.call-start = ((), (), s32[]{:S(2)}) async-start(), calls=%async_computation.3 | async-start | bytes 1769472 | tf_op jit(solution)/shard_map/reduce_scatter | solution.py:26
  358.0 94.5 %all-gather.5.cloned.1.call-start = ((), (), s32[]{:S(2)}) async-start(), calls=%async_computation.4 | async-start | bytes 1671168 | tf_op jit(solution)/shard_map/all_gather | solution.py:32
Sparse Core Ops, SparseCore 0:
  10.5 93.7 all-gather.2
  170.6 187.3 reduce-scatter.6
  360.6 39.5 reduce-scatter.4
  403.3 49.1 all-gather.4
where the time goes:
time: 464 us; the launch traced here: 463 us
  waiting for transfers between devices  377 us (81%)
  matrix products  43.9 us (9%)
  local copies, waits for them, and re-layouts  26.3 us (6%)
  between operations  13.8 us (3%)
    reduce_scatter x1, waiting for transfers between devices, shards(): lax.psum_scatter(partial_value, 'fsdp', scatter_dimension=0, tiled=True)  187 us
    all_gather x1, waiting for transfers between devices, shards(): lax.all_gather(grads_out, 'fsdp', axis=1, tiled=True)  96.3 us
    all_gather x1, waiting for transfers between devices, shards(): full_rank = lax.all_gather(normed, 'fsdp', axis=0, tiled=True)  50.6 us
    reduce_scatter x1, waiting for transfers between devices, shards(): shares = lax.psum_scatter(rowwise, 'dp', scatter_dimension=1, tiled=True)  42.1 us
    dot_general x1, matrix products, shards(): lax.dot_general(basis_wide, lax.dot_general(acts, lax.all_gather(grads_ou...  26.8 us
    unnamed x8, local copies, waits for them, and re-layouts  26.3 us
    dot_general x1, matrix products, shards(): lax.dot_general(acts, lax.all_gather(grads_out, 'fsdp', axis=1, tiled=Tru...  14.7 us
  transfers between devices with their start and end apart: 4, of which 4 were waited for; matrix products, arithmetic and copies ran while one was open for 0% of the time, Pallas kernels for 0%

commit v1 on v0

v1 whole, which is shorter than its diff:
```python
import functools

import jax
import jax.numpy as jnp
from jax import lax
from jax.experimental import pallas as pl
from jax.experimental.pallas import tpu as pltpu
from jax.sharding import PartitionSpec as P

bias_one = 1.0 - 0.9**10
bias_two = 1.0 - 0.999**10
adam_eps = 1e-08
galore_scale = 0.25

MESH = pl.DeviceIdType.MESH
bf16, f32 = jnp.bfloat16, jnp.float32

CHIPS = 8
ROWS = 32
TOK = 512
WIDE = 1536
HALF = WIDE // 2
K = 4
W = WIDE // K


def kernel(
    acts_ref, g_ref, basis_ref, fm_ref, sm_ref,
    upd_ref, m1_ref, m2_ref,
    acts, basis, gfull, fm, sm, upd, m1, m2,
    pown, psend, precv, asend, arecv, pfull,
    q, qrecv, tsend, trecv, nfull,
    lsem, pair_s, pair_r, a_s, a_r, ag_s, ag_r, b_s, b_r, t_s, t_r, c_s, c_r, f_s, f_r,
):
    i, j = lax.axis_index("dp"), lax.axis_index("fsdp")
    m, c = j // 2, j % 2
    other = 1 - c
    pair = (i, 2 * m + other)

    def in_row(d):
        return lax.rem(m + d, CHIPS)

    def in_col(d):
        return lax.rem(i + d, CHIPS)

    def remote(src, dst, s, r, device):
        return pltpu.make_async_remote_copy(
            src_ref=src, dst_ref=dst, send_sem=s, recv_sem=r, device_id=device, device_id_type=MESH
        )

    loads = [
        pltpu.make_async_copy(acts_ref, acts, lsem.at[0]),
        pltpu.make_async_copy(basis_ref, basis, lsem.at[1]),
        pltpu.make_async_copy(g_ref, gfull.at[c], lsem.at[2]),
        pltpu.make_async_copy(fm_ref, fm, lsem.at[3]),
        pltpu.make_async_copy(sm_ref, sm, lsem.at[4]),
    ]
    for load in loads:
        load.start()

    barrier = pltpu.get_barrier_semaphore()
    pl.semaphore_signal(barrier, inc=1, device_id=pair, device_id_type=MESH)
    for d in range(1, CHIPS):
        pl.semaphore_signal(barrier, inc=1, device_id=(i, 2 * in_row(d) + c), device_id_type=MESH)
        pl.semaphore_signal(barrier, inc=1, device_id=(in_col(d), j), device_id_type=MESH)
    turned = (m, 2 * i + c)

    @pl.when(i != m)
    def _():
        pl.semaphore_signal(barrier, inc=1, device_id=turned, device_id_type=MESH)

    loads[0].wait()
    loads[1].wait()
    pown[...] = lax.dot_general(
        basis[...], acts[...], (((0,), (1,)), ((), ())), preferred_element_type=f32
    ).reshape(CHIPS, 2, ROWS, TOK)
    psend[...] = pown[:, pl.ds(other, 1)].reshape(CHIPS, ROWS, TOK).astype(bf16)

    @pl.when(i != m)
    def _():
        pl.semaphore_wait(barrier, 2 * CHIPS)

    @pl.when(i == m)
    def _():
        pl.semaphore_wait(barrier, 2 * CHIPS - 1)

    to_pair = remote(psend, precv, pair_s.at[0], pair_r.at[0], pair)
    to_pair.start()
    loads[2].wait()
    g_pair = remote(gfull.at[c], gfull.at[c], pair_s.at[1], pair_r.at[1], pair)
    g_pair.start()

    to_pair.wait()
    asend[...] = (pown[:, pl.ds(c, 1)].reshape(CHIPS, ROWS, TOK) + precv[...].astype(f32)).astype(bf16)
    a_copies = []
    for d in range(1, CHIPS):
        copy = remote(
            asend.at[in_row(d)], arecv.at[d], a_s.at[d], a_r.at[d], (i, 2 * in_row(d) + c)
        )
        copy.start()
        a_copies.append(copy)
    total = asend[m].astype(f32)
    for d in range(1, CHIPS):
        a_copies[d - 1].wait()
        total += arecv[d].astype(f32)
    pfull[m] = total.astype(bf16)
    ag_copies = []
    for d in range(1, CHIPS):
        copy = remote(
            pfull.at[m], pfull.at[m], ag_s.at[d], ag_r.at[d], (i, 2 * in_row(d) + c)
        )
        copy.start()
        ag_copies.append(copy)
    for d in range(1, CHIPS):
        ag_copies[d - 1].wait()
    g_pair.wait()

    b_copies = []
    for k in range(K):
        half, at = k * W // HALF, (k * W) % HALF
        q[k] = (
            jnp.dot(
                pfull[...].reshape(CHIPS * ROWS, TOK),
                gfull[half, :, at : at + W],
                preferred_element_type=f32,
            )
            .astype(bf16)
            .reshape(CHIPS, ROWS, W)
        )
        row = []
        for d in range(1, CHIPS):
            copy = remote(
                q.at[k, in_col(d)], qrecv.at[k, d], b_s.at[k, d], b_r.at[k, d], (in_col(d), j)
            )
            copy.start()
            row.append(copy)
        b_copies.append(row)
    loads[3].wait()
    loads[4].wait()

    def turn(k):
        return remote(tsend.at[k], trecv.at[k], t_s.at[k], t_r.at[k], turned)

    def reduce(k):
        total = q[k, i].astype(f32)
        for d in range(1, CHIPS):
            b_copies[k][d - 1].wait()
            total += qrecv[k, d].astype(f32)
        tsend[k] = total

        @pl.when(i != m)
        def _():
            turn(k).start()

        @pl.when(i == m)
        def _():
            trecv[k] = total

    c_copies = {}

    def moments(k):
        @pl.when(i != m)
        def _():
            turn(k).wait()

        cols = slice(k * W, (k + 1) * W)
        proj = trecv[k]
        one = 0.9 * fm[:, cols] + 0.1 * proj
        two = 0.999 * sm[:, cols] + 0.001 * proj * proj
        m1[:, cols] = one
        m2[:, cols] = two
        nfull[k, m, c] = (one / bias_one / (jnp.sqrt(two / bias_two) + adam_eps)).astype(bf16)
        mine = nfull.at[k, m, c]
        row = []
        for d in range(1, CHIPS):
            copy = remote(mine, mine, c_s.at[k, d], c_r.at[k, d], (i, 2 * in_row(d) + c))
            copy.start()
            row.append(copy)
        c_copies[k] = row

    f_copies = {}

    def share(k):
        for copy in c_copies[k]:
            copy.wait()
        mine = nfull.at[k, :, c]
        f_copies[k] = remote(mine, mine, f_s.at[k], f_r.at[k], pair)
        f_copies[k].start()

    stores = []

    def update(k):
        f_copies[k].wait()
        cols = slice(k * W, (k + 1) * W)
        upd[:, cols] = (
            galore_scale
            * jnp.dot(
                basis[...], nfull[k].reshape(CHIPS * 2 * ROWS, W), preferred_element_type=f32
            )
        ).astype(bf16)
        store = pltpu.make_async_copy(upd.at[:, cols], upd_ref.at[:, cols], lsem.at[5 + k])
        store.start()
        stores.append(store)

    for step in range(K + 3):
        if step < K:
            reduce(step)
        if 0 <= step - 1 < K:
            moments(step - 1)
            if step - 1 == K - 1:
                for n, (src, dst) in enumerate(((m1, m1_ref), (m2, m2_ref))):
                    store = pltpu.make_async_copy(src, dst, lsem.at[5 + K + n])
                    store.start()
                    stores.append(store)
        if 0 <= step - 2 < K:
            share(step - 2)
        if 0 <= step - 3 < K:
            update(step - 3)
    for store in stores:
        store.wait()


def shards(acts, grads_out, basis, first_moment, second_moment):
    any_space = pl.BlockSpec(memory_space=pl.ANY)
    dma = pltpu.SemaphoreType.DMA
    return pl.pallas_call(
        kernel,
        out_shape=(
            jax.ShapeDtypeStruct((TOK, WIDE), bf16),
            jax.ShapeDtypeStruct((ROWS, WIDE), f32),
            jax.ShapeDtypeStruct((ROWS, WIDE), f32),
        ),
        in_specs=[any_space] * 5,
        out_specs=(any_space,) * 3,
        scratch_shapes=[
            pltpu.VMEM((TOK, 512), bf16),
            pltpu.VMEM((512, 512), bf16),
            pltpu.VMEM((2, TOK, HALF), bf16),
            pltpu.VMEM((ROWS, WIDE), f32),
            pltpu.VMEM((ROWS, WIDE), f32),
            pltpu.VMEM((512, WIDE), bf16),
            pltpu.VMEM((ROWS, WIDE), f32),
            pltpu.VMEM((ROWS, WIDE), f32),
            pltpu.VMEM((CHIPS, 2, ROWS, TOK), f32),
            pltpu.VMEM((CHIPS, ROWS, TOK), bf16),
            pltpu.VMEM((CHIPS, ROWS, TOK), bf16),
            pltpu.VMEM((CHIPS, ROWS, TOK), bf16),
            pltpu.VMEM((CHIPS, ROWS, TOK), bf16),
            pltpu.VMEM((CHIPS, ROWS, TOK), bf16),
            pltpu.VMEM((K, CHIPS, ROWS, W), bf16),
            pltpu.VMEM((K, CHIPS, ROWS, W), bf16),
            pltpu.VMEM((K, ROWS, W), f32),
            pltpu.VMEM((K, ROWS, W), f32),
            pltpu.VMEM((K, CHIPS, 2, ROWS, W), bf16),
            dma((7 + K,)),
            dma((2,)),
            dma((2,)),
            dma((CHIPS,)),
            dma((CHIPS,)),
            dma((CHIPS,)),
            dma((CHIPS,)),
            dma((K, CHIPS)),
            dma((K, CHIPS)),
            dma((K,)),
            dma((K,)),
            dma((K, CHIPS)),
            dma((K, CHIPS)),
            dma((K,)),
            dma((K,)),
        ],
        compiler_params=pltpu.CompilerParams(
            collective_id=0, has_side_effects=True, vmem_limit_bytes=56 * 2**20
        ),
        cost_estimate=pl.CostEstimate(flops=2 * 10**9, bytes_accessed=4 * 2**20, transcendentals=0),
        name="galore_step",
    )(acts, grads_out, basis, first_moment, second_moment)


def solution(mesh):
    return jax.shard_map(
        shards,
        mesh=mesh,
        in_specs=(
            P("dp", "fsdp"),
            P("dp", "fsdp"),
            P("fsdp", None),
            P("fsdp", "dp"),
            P("fsdp", "dp"),
        ),
        out_specs=(P("fsdp", "dp"), P("fsdp", "dp"), P("fsdp", "dp")),
        check_vma=False,
    )
```

time: 464 us -> 64.4 us (0.14)
  waiting for transfers between devices: 377 us -> 0 us
  Pallas kernels: 0 us -> 59.5 us
  matrix products: 43.9 us -> 0 us
  local copies, waits for them, and re-layouts: 26.3 us -> 4.06 us
  between operations: 13.8 us -> 0.66 us
    reduce_scatter x2 -> x0, waiting for transfers between devices: 230 us -> none  [the longest x1 187 us: shards(): lax.psum_scatter(partial_value, 'fsdp', scatter_dimension=0, tiled=True)]
    all_gather x2 -> x0, waiting for transfers between devices: 147 us -> none  [the longest x1 96.3 us: shards(): lax.all_gather(grads_out, 'fsdp', axis=1, tiled=True)]
    pallas_call x0 -> x1, Pallas kernels: none -> 59.5 us  [shards(): pl.pallas_call(kernel, out_shape=(jax.ShapeDtypeStruct((TOK, WIDE), bf16)...]
    dot_general x3 -> x0, matrix products: 43.9 us -> none  [the longest x1 26.8 us: shards(): lax.dot_general(basis_wide, lax.dot_general(acts, lax.all_gather(grads_ou...]
    unnamed x8 -> x7, local copies, waits for them, and re-layouts: 26.3 us -> 4.06 us
  transfers between devices with their start and end apart: 4 -> 0, of which waited for: 4 -> 0; matrix products, arithmetic and copies ran while one was open for 0% -> 0% of each run, Pallas kernels for 0% -> 0%
where the time goes in v1:
time: 64.4 us; the launch traced here: 64.2 us
  Pallas kernels  59.5 us (92%)
  local copies, waits for them, and re-layouts  4.06 us (6%)
  between operations  0.66 us (1%)
    pallas_call x1, Pallas kernels, shards(): pl.pallas_call(kernel, out_shape=(jax.ShapeDtypeStruct((TOK, WIDE), bf16)...  59.5 us
    unnamed x7, local copies, waits for them, and re-layouts  4.06 us

profile of v1, /device:TPU:1, one launch (start us, length us, event | category | flops | bytes accessed | tf_op | source)
XLA Modules:
  0.0 64.2 jit_solution(3599535421001050382)
XLA Ops:
  0.6 59.5 %galore_step.1 = (bf16[512,1536]{1,0:T(8,128)(2,1)}, f32[32,1536]{1,0:T(8,128)}, f32[32,1536]{1,0:T(8,128)}) custom-call(bf16[512,512]{1,0:T(8,128)(2,1)} %acts_ref.1, bf16[512,768]{1,0:T(8,128)(2,1)} %g_ref.1, bf16[512,512]{1,0:T(8,128)(2,1)} %basis_ref.1, f32[32,1536]{1,0:T(8,128)} %fm_ref.1, f32[32,1536]{1,0:T(8,128)} %sm_ref.1), custom_call_target="tpu_custom_call" | custom-call | flops 2000000000 | bytes 4194304 | tf_op jit(solution)/shard_map/galore_step/pallas_call | solution.py:226
  60.1 0.0 copy-start.1
  60.1 0.0 copy-start
  60.1 2.7 %copy.11 = bf16[512,1536]{1,0:T(8,128)(2,1)} copy(bf16[512,1536]{1,0:T(8,128)(2,1)} %get-tuple-element.6) | data formatting | bytes 3145728
  62.8 0.0 copy-done.1
  62.8 0.7 %copy.12 = f32[32,1536]{1,0:T(8,128)} copy(f32[32,1536]{1,0:T(8,128)S(1)} %copy-done.1) | data formatting | bytes 393216
  63.5 0.0 copy-done
  63.5 0.7 %copy.13 = f32[32,1536]{1,0:T(8,128)} copy(f32[32,1536]{1,0:T(8,128)S(1)} %copy-done) | data formatting | bytes 393216
Async XLA Ops:
  60.1 2.7 %copy-start.1 = (f32[32,1536]{1,0:T(8,128)S(1)}, f32[32,1536]{1,0:T(8,128)}, u32[]{:S(2)}) copy-start(f32[32,1536]{1,0:T(8,128)} %get-tuple-element.7) | copy-start | bytes 589828
  60.1 3.4 %copy-start = (f32[32,1536]{1,0:T(8,128)S(1)}, f32[32,1536]{1,0:T(8,128)}, u32[]{:S(2)}) copy-start(f32[32,1536]{1,0:T(8,128)} %get-tuple-element.8) | copy-start | bytes 589828

commit v2 on v0

v2 whole, which is shorter than its diff:
```python
import jax
import jax.numpy as jnp
from jax import lax
from jax.experimental import pallas as pl
from jax.experimental.pallas import tpu as pltpu
from jax.sharding import PartitionSpec as P

bias_one = 1.0 - 0.9**10
bias_two = 1.0 - 0.999**10
adam_eps = 1e-08
galore_scale = 0.25

MESH = pl.DeviceIdType.MESH
bf16, f32 = jnp.bfloat16, jnp.float32

CHIPS = 8
ROWS = 32
TOK = 512
DEEP = 512
WIDE = 1536
HALF = WIDE // 2
R = 2
RR = ROWS // R
K = 2
DIRECT = range(99)
W = WIDE // K
PARTS = [(r, k) for r in range(R) for k in range(K)]
LAGS = {"reduce": 0.0, "moments": 3.9, "forward": 6.6, "near": 6.9, "far": 9.3}
GAP = 8.4 / len(PARTS)
STEPS = sorted((lag + GAP * t, name, t) for name, lag in LAGS.items() for t in range(len(PARTS)))


def kernel(
    acts_ref, g_ref, basis_ref, fm_ref, sm_ref,
    upd_ref, m1_ref, m2_ref,
    acts, basis, g, fm, sm, upd, m1, m2,
    pown, psend, precv, asend, arecv, pfull,
    q, qrecv, tsend, trecv, nfull,
    lsem, p_s, p_r, g_s, g_r, a_s, a_r, ag_s, ag_r, b_s, b_r, t_s, t_r,
    c_s, c_r, z_s, z_r, d_s, d_r, f_s, f_r,
):
    i, j = lax.axis_index("dp"), lax.axis_index("fsdp")
    m, c = j // 2, lax.rem(j, 2)
    other = 1 - c
    y, z_lo, z_hi, x = i // 2, lax.rem(i, 2), m // 4, lax.rem(m, 4)
    pair = (i, 2 * m + other)

    rows = [lax.rem(m + d, CHIPS) for d in range(CHIPS)]
    cols_of = [lax.rem(i + d, CHIPS) for d in range(CHIPS)]
    along = [4 * z_hi + lax.rem(x + d, 4) for d in range(4)]
    over = lax.rem(m + 4, CHIPS)
    row_peers = [(i, 2 * to + c) for to in rows]
    col_peers = [(to, j) for to in cols_of]

    def block_of(at):
        x_to = lax.rem(x + 6 + at // 2 - 2 * z_hi - x // 2, 4)
        return 4 * lax.rem(z_hi + at + x, 2) + x_to

    blocks = [block_of(to) for to in cols_of]
    row_to = blocks[0]
    z_from, x_from = i // 4, lax.rem(i, 4)
    y_from = lax.rem(x + 6 - x_from + 2 * z_from + x_from // 2, 4)
    i_from = 2 * y_from + lax.rem(z_hi + z_from + x_from, 2)
    stays = jnp.logical_and(m == i, row_to == m)
    turned, comes = (m, 2 * row_to + c), (i_from, 2 * i + c)

    def remote(src, dst, s, r, device):
        return pltpu.make_async_remote_copy(
            src_ref=src, dst_ref=dst, send_sem=s, recv_sem=r, device_id=device, device_id_type=MESH
        )

    sent = []

    def got(copy):
        copy.wait_recv()
        sent.append(copy)

    g_here = g.at[:, pl.ds(pl.multiple_of(c * HALF, HALF), HALF)]
    loads = [
        pltpu.make_async_copy(acts_ref, acts, lsem.at[0]),
        pltpu.make_async_copy(basis_ref, basis, lsem.at[1]),
        pltpu.make_async_copy(g_ref, g_here, lsem.at[2]),
        pltpu.make_async_copy(fm_ref, fm, lsem.at[3]),
        pltpu.make_async_copy(sm_ref, sm, lsem.at[4]),
    ]
    for load in loads:
        load.start()

    barrier = pltpu.get_barrier_semaphore()
    pl.semaphore_signal(barrier, inc=1, device_id=pair, device_id_type=MESH)
    for d in range(1, CHIPS):
        pl.semaphore_signal(barrier, inc=1, device_id=row_peers[d], device_id_type=MESH)
        pl.semaphore_signal(barrier, inc=1, device_id=col_peers[d], device_id_type=MESH)

    @pl.when(jnp.logical_not(stays))
    def _():
        pl.semaphore_signal(barrier, inc=1, device_id=turned, device_id_type=MESH)
        pl.semaphore_signal(barrier, inc=1, device_id=comes, device_id_type=MESH)

    loads[0].wait()
    loads[1].wait()
    pown[...] = lax.dot_general(
        basis[...], acts[...], (((0,), (1,)), ((), ())), preferred_element_type=f32
    ).reshape(CHIPS, 2, ROWS, TOK)
    for r in range(R):
        psend[r] = pown[:, pl.ds(other, 1), r * RR : (r + 1) * RR].reshape(CHIPS, RR, TOK).astype(bf16)

    @pl.when(jnp.logical_not(stays))
    def _():
        pl.semaphore_wait(barrier, 2 * CHIPS + 1)

    @pl.when(stays)
    def _():
        pl.semaphore_wait(barrier, 2 * CHIPS - 1)

    to_pair = [remote(psend.at[r], precv.at[r], p_s.at[r], p_r.at[r], pair) for r in range(R)]
    for copy in to_pair:
        copy.start()
    loads[2].wait()
    g_pair = remote(g_here, g_here, g_s.at[0], g_r.at[0], pair)
    g_pair.start()

    a_copies = [
        [
            remote(
                asend.at[r, rows[d]],
                arecv.at[r, d],
                a_s.at[r, d],
                a_r.at[r, d],
                row_peers[d],
            )
            for d in range(1, CHIPS)
        ]
        for r in range(R)
    ]
    for r in range(R):
        got(to_pair[r])
        asend[r] = (
            pown[:, pl.ds(c, 1), r * RR : (r + 1) * RR].reshape(CHIPS, RR, TOK)
            + precv[r].astype(f32)
        ).astype(bf16)
        for copy in a_copies[r]:
            copy.start()
    ag_copies = [
        [
            remote(
                pfull.at[r, m],
                pfull.at[r, m],
                ag_s.at[r, d],
                ag_r.at[r, d],
                row_peers[d],
            )
            for d in range(1, CHIPS)
        ]
        for r in range(R)
    ]
    for r in range(R):
        total = asend[r, m].astype(f32)
        for d in range(1, CHIPS):
            got(a_copies[r][d - 1])
            total += arecv[r, d].astype(f32)
        pfull[r, m] = total.astype(bf16)
        for copy in ag_copies[r]:
            copy.start()

    b_copies = []
    for t, (r, k) in enumerate(PARTS):
        if k == 0:
            for copy in ag_copies[r]:
                got(copy)
        if t == 0:
            got(g_pair)
        q[t] = (
            jnp.dot(
                pfull[r].reshape(CHIPS * RR, TOK),
                g[:, k * W : (k + 1) * W],
                preferred_element_type=f32,
            )
            .astype(bf16)
            .reshape(CHIPS, RR, W)
        )
        b_copies.append(
            [
                remote(
                    q.at[t, blocks[d]],
                    qrecv.at[t, d],
                    b_s.at[t, d],
                    b_r.at[t, d],
                    col_peers[d],
                )
                for d in range(1, CHIPS)
            ]
        )
        for copy in b_copies[t]:
            copy.start()
    loads[3].wait()
    loads[4].wait()

    def turn(t):
        return remote(tsend.at[t], trecv.at[t], t_s.at[t], t_r.at[t], turned)

    def reduce(t):
        total = q[t, row_to].astype(f32)
        for d in range(1, CHIPS):
            got(b_copies[t][d - 1])
            total += qrecv[t, d].astype(f32)
        tsend[t] = total.astype(bf16)

        @pl.when(jnp.logical_not(stays))
        def _():
            turn(t).start()

        @pl.when(stays)
        def _():
            trecv[t] = total.astype(bf16)

    near_copies, far_copies, shares = {}, {}, {}
    lines = [slice(r * RR, (r + 1) * RR) for r in range(R)]

    def along_x(t, chip, s, r):
        block = nfull.at[PARTS[t][1], chip, c, lines[PARTS[t][0]]]
        copies = []
        for d in range(1, 4):
            copies.append(remote(block, block, s.at[t, d], r.at[t, d], (i, 2 * along[d] + c)))
            copies[-1].start()
        return copies

    def beyond(t):
        block = nfull.at[PARTS[t][1], m, c, lines[PARTS[t][0]]]
        copies = []
        for d in range(1, 4):
            to = lax.rem(along[d] + 4, CHIPS)
            copies.append(remote(block, block, d_s.at[t, d], d_r.at[t, d], (i, 2 * to + c)))
            copies[-1].start()
        return copies

    def across(t):
        mine = nfull.at[PARTS[t][1], m, c, lines[PARTS[t][0]]]
        return remote(mine, mine, z_s.at[t], z_r.at[t], (i, 2 * over + c))

    def to_other_core(t, first, n):
        part = nfull.at[PARTS[t][1], pl.ds(first, 4), c, lines[PARTS[t][0]]]
        shares[t, n] = remote(part, part, f_s.at[t, n], f_r.at[t, n], pair)
        shares[t, n].start()

    def moments(t):
        @pl.when(jnp.logical_not(stays))
        def _():
            turn(t).wait_recv()

        r, k = PARTS[t]
        cols = slice(k * W, (k + 1) * W)
        proj = trecv[t].astype(f32)
        one = 0.9 * fm[lines[r], cols] + 0.1 * proj
        two = 0.999 * sm[lines[r], cols] + 0.001 * proj * proj
        nfull[k, m, c, lines[r]] = (
            one / bias_one / (jnp.sqrt(two / bias_two) + adam_eps)
        ).astype(bf16)
        across(t).start()
        near_copies[t] = along_x(t, m, c_s, c_r)
        if t in DIRECT:
            far_copies[t] = beyond(t)
        m1[lines[r], cols] = one
        m2[lines[r], cols] = two

    def forward(t):
        if t not in DIRECT:
            got(across(t))
            far_copies[t] = along_x(t, over, d_s, d_r)

    def near(t):
        for copy in near_copies[t]:
            got(copy)
        to_other_core(t, 4 * z_hi, 0)

    stores = []

    def store(src, dst):
        stores.append(pltpu.make_async_copy(src, dst, lsem.at[5 + len(stores)]))
        stores[-1].start()

    def far(t):
        if t in DIRECT:
            got(across(t))
        for copy in far_copies[t]:
            got(copy)
        to_other_core(t, 4 * (1 - z_hi), 1)

    def update(k):
        for t in range(len(PARTS)):
            if PARTS[t][1] == k:
                got(shares[t, 0])
                got(shares[t, 1])
        cols = slice(k * W, (k + 1) * W)
        upd[:, cols] = (
            galore_scale
            * jnp.dot(
                basis[...], nfull[k].reshape(CHIPS * 2 * ROWS, W), preferred_element_type=f32
            )
        ).astype(bf16)
        store(upd.at[:, cols], upd_ref.at[:, cols])

    steps = {"reduce": reduce, "moments": moments, "forward": forward, "near": near, "far": far}
    pending = []
    for _, name, t in STEPS:
        steps[name](t)
        if (name, t) == ("moments", len(PARTS) - 1):
            store(m1, m1_ref)
            store(m2, m2_ref)
        if pending and name in ("near", "far"):
            update(pending.pop())
        if name == "far" and PARTS[t][0] == R - 1:
            pending.append(PARTS[t][1])
    for k in pending:
        update(k)
    for copy in stores:
        copy.wait()
    for copy in sent:
        copy.wait_send()

    @pl.when(jnp.logical_not(stays))
    def _():
        for t in range(len(PARTS)):
            turn(t).wait_send()


def shards(acts, grads_out, basis, first_moment, second_moment):
    def vmem(shape, dtype):
        return pltpu.VMEM(shape, dtype)

    def dma(*shape):
        return pltpu.SemaphoreType.DMA(shape)

    n = len(PARTS)
    return pl.pallas_call(
        kernel,
        out_shape=(
            jax.ShapeDtypeStruct((DEEP, WIDE), bf16),
            jax.ShapeDtypeStruct((ROWS, WIDE), f32),
            jax.ShapeDtypeStruct((ROWS, WIDE), f32),
        ),
        in_specs=[pl.BlockSpec(memory_space=IN_SPACE)] * 5,
        out_specs=(pl.BlockSpec(memory_space=pl.ANY),) * 3,
        scratch_shapes=[
            vmem((TOK, DEEP), bf16),
            vmem((DEEP, 512), bf16),
            vmem((TOK, WIDE), bf16),
            vmem((ROWS, WIDE), f32),
            vmem((ROWS, WIDE), f32),
            vmem((DEEP, WIDE), bf16),
            vmem((ROWS, WIDE), f32),
            vmem((ROWS, WIDE), f32),
            vmem((CHIPS, 2, ROWS, TOK), f32),
            vmem((R, CHIPS, RR, TOK), bf16),
            vmem((R, CHIPS, RR, TOK), bf16),
            vmem((R, CHIPS, RR, TOK), bf16),
            vmem((R, CHIPS, RR, TOK), bf16),
            vmem((R, CHIPS, RR, TOK), bf16),
            vmem((n, CHIPS, RR, W), bf16),
            vmem((n, CHIPS, RR, W), bf16),
            vmem((n, RR, W), bf16),
            vmem((n, RR, W), bf16),
            vmem((K, CHIPS, 2, ROWS, W), bf16),
            dma(7 + K),
            dma(R),
            dma(R),
            dma(1),
            dma(1),
            dma(R, CHIPS),
            dma(R, CHIPS),
            dma(R, CHIPS),
            dma(R, CHIPS),
            dma(n, CHIPS),
            dma(n, CHIPS),
            dma(n),
            dma(n),
            dma(n, 4),
            dma(n, 4),
            dma(n),
            dma(n),
            dma(n, 4),
            dma(n, 4),
            dma(n, 2),
            dma(n, 2),
        ],
        compiler_params=pltpu.CompilerParams(
            collective_id=0, has_side_effects=True, vmem_limit_bytes=LIMIT * 2**20
        ),
        cost_estimate=pl.CostEstimate(flops=2 * 10**9, bytes_accessed=4 * 2**20, transcendentals=0),
        name="galore_step",
    )(*(pltpu.with_memory_space_constraint(v, pltpu.HBM) for v in (acts, grads_out, basis, first_moment, second_moment)))


IN_SPACE = pl.ANY
LIMIT = 24


def solution(mesh):
    return jax.shard_map(
        shards,
        mesh=mesh,
        in_specs=(
            P("dp", "fsdp"),
            P("dp", "fsdp"),
            P("fsdp", None),
            P("fsdp", "dp"),
            P("fsdp", "dp"),
        ),
        out_specs=(P("fsdp", "dp"), P("fsdp", "dp"), P("fsdp", "dp")),
        check_vma=False,
    )
```

time: 464 us -> 52.6 us (0.11)
  waiting for transfers between devices: 377 us -> 0 us
  Pallas kernels: 0 us -> 49.3 us
  matrix products: 43.9 us -> 0 us
  local copies, waits for them, and re-layouts: 26.3 us -> 2.5 us
  between operations: 13.8 us -> 0.64 us
    reduce_scatter x2 -> x0, waiting for transfers between devices: 230 us -> none  [the longest x1 187 us: shards(): lax.psum_scatter(partial_value, 'fsdp', scatter_dimension=0, tiled=True)]
    all_gather x2 -> x0, waiting for transfers between devices: 147 us -> none  [the longest x1 96.3 us: shards(): lax.all_gather(grads_out, 'fsdp', axis=1, tiled=True)]
    pallas_call x0 -> x1, Pallas kernels: none -> 49.3 us  [shards(): pl.pallas_call(kernel, out_shape=(jax.ShapeDtypeStruct((DEEP, WIDE), bf16...]
    dot_general x3 -> x0, matrix products: 43.9 us -> none  [the longest x1 26.8 us: shards(): lax.dot_general(basis_wide, lax.dot_general(acts, lax.all_gather(grads_ou...]
    unnamed x8 -> x3, local copies, waits for them, and re-layouts: 26.3 us -> 2.5 us
  transfers between devices with their start and end apart: 4 -> 0, of which waited for: 4 -> 0; matrix products, arithmetic and copies ran while one was open for 0% -> 0% of each run, Pallas kernels for 0% -> 0%
where the time goes in v2:
time: 52.6 us; the launch traced here: 52.5 us
  Pallas kernels  49.3 us (94%)
  local copies, waits for them, and re-layouts  2.5 us (5%)
  between operations  0.64 us (1%)
    pallas_call x1, Pallas kernels, shards(): pl.pallas_call(kernel, out_shape=(jax.ShapeDtypeStruct((DEEP, WIDE), bf16...  49.3 us
    unnamed x3, local copies, waits for them, and re-layouts  2.5 us

profile of v2, /device:TPU:1, one launch (start us, length us, event | category | flops | bytes accessed | tf_op | source)
XLA Modules:
  0.0 52.5 jit_solution(12792991892036799149)
XLA Ops:
  0.6 49.3 %galore_step.1 = (bf16[512,1536]{1,0:T(8,128)(2,1)S(1)}, f32[32,1536]{1,0:T(8,128)S(1)}, f32[32,1536]{1,0:T(8,128)S(1)}) custom-call(bf16[512,512]{1,0:T(8,128)(2,1)} %acts_ref.1, bf16[512,768]{1,0:T(8,128)(2,1)} %g_ref.1, bf16[512,512]{1,0:T(8,128)(2,1)} %basis_ref.1, f32[32,1536]{1,0:T(8,128)} %fm_ref.1, f32[32,1536]{1,0:T(8,128)} %sm_ref.1), custom_call_target="tpu_custom_call" | custom-call | flops 2000000000 | bytes 4194304 | tf_op jit(solution)/shard_map/galore_step/pallas_call | solution.py:335
  50.0 1.1 %copy.11 = bf16[512,1536]{1,0:T(8,128)(2,1)} copy(bf16[512,1536]{1,0:T(8,128)(2,1)S(1)} %get-tuple-element.6) | data formatting | bytes 3145728
  51.1 0.7 %copy.12 = f32[32,1536]{1,0:T(8,128)} copy(f32[32,1536]{1,0:T(8,128)S(1)} %get-tuple-element.7) | data formatting | bytes 393216
  51.8 0.7 %copy.13 = f32[32,1536]{1,0:T(8,128)} copy(f32[32,1536]{1,0:T(8,128)S(1)} %get-tuple-element.8) | data formatting | bytes 393216

commit v3 on v2

--- a/solution.py
+++ b/solution.py
@@ -22,18 +22,23 @@
 R = 2
 RR = ROWS // R
 K = 2
-DIRECT = range(99)
 W = WIDE // K
 PARTS = [(r, k) for r in range(R) for k in range(K)]
-LAGS = {"reduce": 0.0, "moments": 3.9, "forward": 6.6, "near": 6.9, "far": 9.3}
+LAGS = {"reduce": 0.0, "moments": 3.9, "near": 6.9, "far": 9.3}
+FLUSH = {("reduce", 3), ("moments", 3), ("far", 3)}
+FAR_FIRST = [(0, 0), (1, 2), (1, 1), (1, 3), (0, 2), (1, 0), (0, 1), (0, 3)]
 GAP = 8.4 / len(PARTS)
 STEPS = sorted((lag + GAP * t, name, t) for name, lag in LAGS.items() for t in range(len(PARTS)))
 
 
+def new_moments(first, second, proj):
+    return 0.9 * first + 0.1 * proj, 0.999 * second + 0.001 * proj * proj
+
+
 def kernel(
     acts_ref, g_ref, basis_ref, fm_ref, sm_ref,
-    upd_ref, m1_ref, m2_ref,
-    acts, basis, g, fm, sm, upd, m1, m2,
+    upd, proj_ref,
+    acts, basis, g, fm, sm,
     pown, psend, precv, asend, arecv, pfull,
     q, qrecv, tsend, trecv, nfull,
     lsem, p_s, p_r, g_s, g_r, a_s, a_r, ag_s, ag_r, b_s, b_r, t_s, t_r,
@@ -45,8 +50,8 @@
     y, z_lo, z_hi, x = i // 2, lax.rem(i, 2), m // 4, lax.rem(m, 4)
     pair = (i, 2 * m + other)
 
-    rows = [lax.rem(m + d, CHIPS) for d in range(CHIPS)]
-    cols_of = [lax.rem(i + d, CHIPS) for d in range(CHIPS)]
+    rows = [4 * lax.rem(z_hi + dz, 2) + lax.rem(x + dx, 4) for dz, dx in FAR_FIRST]
+    cols_of = [2 * lax.rem(y + dy, 4) + lax.rem(z_lo + dz, 2) for dz, dy in FAR_FIRST]
     along = [4 * z_hi + lax.rem(x + d, 4) for d in range(4)]
     over = lax.rem(m + 4, CHIPS)
     row_peers = [(i, 2 * to + c) for to in rows]
@@ -74,6 +79,10 @@
     def got(copy):
         copy.wait_recv()
         sent.append(copy)
+
+    def flush():
+        while sent:
+            sent.pop(0).wait_send()
 
     g_here = g.at[:, pl.ds(pl.multiple_of(c * HALF, HALF), HALF)]
     loads = [
@@ -87,7 +96,6 @@
         load.start()
 
     barrier = pltpu.get_barrier_semaphore()
-    pl.semaphore_signal(barrier, inc=1, device_id=pair, device_id_type=MESH)
     for d in range(1, CHIPS):
         pl.semaphore_signal(barrier, inc=1, device_id=row_peers[d], device_id_type=MESH)
         pl.semaphore_signal(barrier, inc=1, device_id=col_peers[d], device_id_type=MESH)
@@ -96,6 +104,8 @@
     def _():
         pl.semaphore_signal(barrier, inc=1, device_id=turned, device_id_type=MESH)
         pl.semaphore_signal(barrier, inc=1, device_id=comes, device_id_type=MESH)
+
+    pl.semaphore_signal(barrier, inc=1, device_id=pair, device_id_type=MESH)
 
     loads[0].wait()
     loads[1].wait()
@@ -195,6 +205,7 @@
             copy.start()
     loads[3].wait()
     loads[4].wait()
+    flush()
 
     def turn(t):
         return remote(tsend.at[t], trecv.at[t], t_s.at[t], t_r.at[t], turned)
@@ -217,18 +228,18 @@
     near_copies, far_copies, shares = {}, {}, {}
     lines = [slice(r * RR, (r + 1) * RR) for r in range(R)]
 
-    def along_x(t, chip, s, r):
-        block = nfull.at[PARTS[t][1], chip, c, lines[PARTS[t][0]]]
+    def along_x(t):
+        block = nfull.at[PARTS[t][1], m, c, lines[PARTS[t][0]]]
         copies = []
-        for d in range(1, 4):
-            copies.append(remote(block, block, s.at[t, d], r.at[t, d], (i, 2 * along[d] + c)))
+        for d in (2, 1, 3):
+            copies.append(remote(block, block, c_s.at[t, d], c_r.at[t, d], (i, 2 * along[d] + c)))
             copies[-1].start()
         return copies
 
     def beyond(t):
         block = nfull.at[PARTS[t][1], m, c, lines[PARTS[t][0]]]
         copies = []
-        for d in range(1, 4):
+        for d in (2, 1, 3):
             to = lax.rem(along[d] + 4, CHIPS)
             copies.append(remote(block, block, d_s.at[t, d], d_r.at[t, d], (i, 2 * to + c)))
             copies[-1].start()
@@ -251,37 +262,22 @@
         r, k = PARTS[t]
         cols = slice(k * W, (k + 1) * W)
         proj = trecv[t].astype(f32)
-        one = 0.9 * fm[lines[r], cols] + 0.1 * proj
-        two = 0.999 * sm[lines[r], cols] + 0.001 * proj * proj
+        one, two = new_moments(fm[lines[r], cols], sm[lines[r], cols], proj)
         nfull[k, m, c, lines[r]] = (
             one / bias_one / (jnp.sqrt(two / bias_two) + adam_eps)
         ).astype(bf16)
+        far_copies[t] = beyond(t)
         across(t).start()
-        near_copies[t] = along_x(t, m, c_s, c_r)
-        if t in DIRECT:
-            far_copies[t] = beyond(t)
-        m1[lines[r], cols] = one
-        m2[lines[r], cols] = two
-
-    def forward(t):
-        if t not in DIRECT:
-            got(across(t))
-            far_copies[t] = along_x(t, over, d_s, d_r)
+        near_copies[t] = along_x(t)
+        proj_ref[lines[r], cols] = proj
 
     def near(t):
         for copy in near_copies[t]:
             got(copy)
         to_other_core(t, 4 * z_hi, 0)
 
-    stores = []
-
-    def store(src, dst):
-        stores.append(pltpu.make_async_copy(src, dst, lsem.at[5 + len(stores)]))
-        stores[-1].start()
-
     def far(t):
-        if t in DIRECT:
-            got(across(t))
+        got(across(t))
         for copy in far_copies[t]:
             got(copy)
         to_other_core(t, 4 * (1 - z_hi), 1)
@@ -298,25 +294,20 @@
                 basis[...], nfull[k].reshape(CHIPS * 2 * ROWS, W), preferred_element_type=f32
             )
         ).astype(bf16)
-        store(upd.at[:, cols], upd_ref.at[:, cols])
-
-    steps = {"reduce": reduce, "moments": moments, "forward": forward, "near": near, "far": far}
+
+    steps = {"reduce": reduce, "moments": moments, "near": near, "far": far}
     pending = []
     for _, name, t in STEPS:
         steps[name](t)
-        if (name, t) == ("moments", len(PARTS) - 1):
-            store(m1, m1_ref)
-            store(m2, m2_ref)
+        if (name, t) in FLUSH:
+            flush()
         if pending and name in ("near", "far"):
             update(pending.pop())
         if name == "far" and PARTS[t][0] == R - 1:
             pending.append(PARTS[t][1])
     for k in pending:
         update(k)
-    for copy in stores:
-        copy.wait()
-    for copy in sent:
-        copy.wait_send()
+    flush()
 
     @pl.when(jnp.logical_not(stays))
     def _():
@@ -332,24 +323,20 @@
         return pltpu.SemaphoreType.DMA(shape)
 
     n = len(PARTS)
-    return pl.pallas_call(
+    update, proj = pl.pallas_call(
         kernel,
         out_shape=(
             jax.ShapeDtypeStruct((DEEP, WIDE), bf16),
             jax.ShapeDtypeStruct((ROWS, WIDE), f32),
-            jax.ShapeDtypeStruct((ROWS, WIDE), f32),
         ),
         in_specs=[pl.BlockSpec(memory_space=IN_SPACE)] * 5,
-        out_specs=(pl.BlockSpec(memory_space=pl.ANY),) * 3,
+        out_specs=(pl.BlockSpec(memory_space=pltpu.VMEM),) * 2,
         scratch_shapes=[
             vmem((TOK, DEEP), bf16),
             vmem((DEEP, 512), bf16),
             vmem((TOK, WIDE), bf16),
             vmem((ROWS, WIDE), f32),
             vmem((ROWS, WIDE), f32),
-            vmem((DEEP, WIDE), bf16),
-            vmem((ROWS, WIDE), f32),
-            vmem((ROWS, WIDE), f32),
             vmem((CHIPS, 2, ROWS, TOK), f32),
             vmem((R, CHIPS, RR, TOK), bf16),
             vmem((R, CHIPS, RR, TOK), bf16),
@@ -361,7 +348,7 @@
             vmem((n, RR, W), bf16),
             vmem((n, RR, W), bf16),
             vmem((K, CHIPS, 2, ROWS, W), bf16),
-            dma(7 + K),
+            dma(5),
             dma(R),
             dma(R),
             dma(1),
@@ -389,6 +376,7 @@
         cost_estimate=pl.CostEstimate(flops=2 * 10**9, bytes_accessed=4 * 2**20, transcendentals=0),
         name="galore_step",
     )(*(pltpu.with_memory_space_constraint(v, pltpu.HBM) for v in (acts, grads_out, basis, first_moment, second_moment)))
+    return update, *new_moments(first_moment, second_moment, proj)
 
 
 IN_SPACE = pl.ANY

time: 52.6 us -> 49.4 us (0.939)
  Pallas kernels: 49.3 us -> 46.5 us
  local copies, waits for them, and re-layouts: 2.5 us -> 1.15 us
  other arithmetic: 0 us -> 0.8 us
    pallas_call x1, Pallas kernels: 49.3 us -> 46.5 us  [shards(): pl.pallas_call(kernel, out_shape=(jax.ShapeDtypeStruct((DEEP, WIDE), bf16...]
    unnamed x3 -> x5, local copies, waits for them, and re-layouts: 2.5 us -> 1.15 us
    add x0 -> x1, other arithmetic: none -> 0.8 us  [new_moments(): return (0.9 * first + 0.1 * proj, 0.999 * second + 0.001 * proj * proj)]
where the time goes in v3:
time: 49.4 us; the launch traced here: 49.1 us
  Pallas kernels  46.5 us (94%)
  local copies, waits for them, and re-layouts  1.15 us (2%)
  other arithmetic  0.8 us (2%)
  between operations  0.67 us (1%)
    pallas_call x1, Pallas kernels, shards(): pl.pallas_call(kernel, out_shape=(jax.ShapeDtypeStruct((DEEP, WIDE), bf16...  46.5 us
    unnamed x5, local copies, waits for them, and re-layouts  1.15 us

profile of v3, /device:TPU:1, one launch (start us, length us, event | category | flops | bytes accessed | tf_op | source)
XLA Modules:
  0.0 49.1 jit_solution(12331500170429748116)
XLA Ops:
  0.6 0.0 copy-start.1
  0.6 0.0 copy-start
  0.7 46.5 %galore_step.1 = (bf16[512,1536]{1,0:T(8,128)(2,1)S(1)}, f32[32,1536]{1,0:T(8,128)S(1)}) custom-call(bf16[512,512]{1,0:T(8,128)(2,1)} %acts_ref.1, bf16[512,768]{1,0:T(8,128)(2,1)} %g_ref.1, bf16[512,512]{1,0:T(8,128)(2,1)} %basis_ref.1, f32[32,1536]{1,0:T(8,128)} %fm_ref.1, f32[32,1536]{1,0:T(8,128)} %sm_ref.1), custom_call_target="tpu_custom_call" | custom-call | flops 2000000000 | bytes 4194304 | tf_op jit(solution)/shard_map/galore_step/pallas_call | solution.py:326
  47.1 0.0 copy-done.1
  47.2 0.0 copy-done
  47.2 0.8 %fusion = (f32[32,1536]{1,0:T(8,128)}, f32[32,1536]{1,0:T(8,128)}) fusion(f32[32,1536]{1,0:T(8,128)S(1)} %get-tuple-element.6, f32[32,1536]{1,0:T(8,128)S(1)} %copy-done.1, f32[32,1536]{1,0:T(8,128)S(1)} %copy-done), kind=kLoop, calls=%fused_computation.1 | loop fusion | flops 344064 | bytes 983040 | tf_op jit(solution)/shard_map/add | solution.py:35
  48.0 1.1 %copy.9 = bf16[512,1536]{1,0:T(8,128)(2,1)} copy(bf16[512,1536]{1,0:T(8,128)(2,1)S(1)} %get-tuple-element.12) | data formatting | bytes 3145728
Async XLA Ops:
  0.6 46.5 %copy-start.1 = (f32[32,1536]{1,0:T(8,128)S(1)}, f32[32,1536]{1,0:T(8,128)}, u32[]{:S(2)}) copy-start(f32[32,1536]{1,0:T(8,128)} %sm_ref.1) | copy-start | bytes 589828
  0.6 46.5 %copy-start = (f32[32,1536]{1,0:T(8,128)S(1)}, f32[32,1536]{1,0:T(8,128)}, u32[]{:S(2)}) copy-start(f32[32,1536]{1,0:T(8,128)} %fm_ref.1) | copy-start | bytes 589828

commit v4 on v3

--- a/solution.py
+++ b/solution.py
@@ -42,7 +42,7 @@
     pown, psend, precv, asend, arecv, pfull,
     q, qrecv, tsend, trecv, nfull,
     lsem, p_s, p_r, g_s, g_r, a_s, a_r, ag_s, ag_r, b_s, b_r, t_s, t_r,
-    c_s, c_r, z_s, z_r, d_s, d_r, f_s, f_r,
+    c_s, c_r, d_s, d_r, f_s, f_r,
 ):
     i, j = lax.axis_index("dp"), lax.axis_index("fsdp")
     m, c = j // 2, lax.rem(j, 2)
@@ -79,6 +79,9 @@
     def got(copy):
         copy.wait_recv()
         sent.append(copy)
+
+    def got_all(ref, s, r):
+        got(remote(ref, ref, s, r, pair))
 
     def flush():
         while sent:
@@ -135,8 +138,8 @@
             remote(
                 asend.at[r, rows[d]],
                 arecv.at[r, d],
-                a_s.at[r, d],
-                a_r.at[r, d],
+                a_s.at[r],
+                a_r.at[r],
                 row_peers[d],
             )
             for d in range(1, CHIPS)
@@ -156,8 +159,8 @@
             remote(
                 pfull.at[r, m],
                 pfull.at[r, m],
-                ag_s.at[r, d],
-                ag_r.at[r, d],
+                ag_s.at[r],
+                ag_r.at[r],
                 row_peers[d],
             )
             for d in range(1, CHIPS)
@@ -166,8 +169,8 @@
     ]
     for r in range(R):
         total = asend[r, m].astype(f32)
+        got_all(arecv.at[r, pl.ds(1, CHIPS - 1)], a_s.at[r], a_r.at[r])
         for d in range(1, CHIPS):
-            got(a_copies[r][d - 1])
             total += arecv[r, d].astype(f32)
         pfull[r, m] = total.astype(bf16)
         for copy in ag_copies[r]:
@@ -176,8 +179,7 @@
     b_copies = []
     for t, (r, k) in enumerate(PARTS):
         if k == 0:
-            for copy in ag_copies[r]:
-                got(copy)
+            got_all(arecv.at[r, pl.ds(1, CHIPS - 1)], ag_s.at[r], ag_r.at[r])
         if t == 0:
             got(g_pair)
         q[t] = (
@@ -194,8 +196,8 @@
                 remote(
                     q.at[t, blocks[d]],
                     qrecv.at[t, d],
-                    b_s.at[t, d],
-                    b_r.at[t, d],
+                    b_s.at[t],
+                    b_r.at[t],
                     col_peers[d],
                 )
                 for d in range(1, CHIPS)
@@ -212,8 +214,8 @@
 
     def reduce(t):
         total = q[t, row_to].astype(f32)
+        got_all(qrecv.at[t, pl.ds(1, CHIPS - 1)], b_s.at[t], b_r.at[t])
         for d in range(1, CHIPS):
-            got(b_copies[t][d - 1])
             total += qrecv[t, d].astype(f32)
         tsend[t] = total.astype(bf16)
 
@@ -232,7 +234,7 @@
         block = nfull.at[PARTS[t][1], m, c, lines[PARTS[t][0]]]
         copies = []
         for d in (2, 1, 3):
-            copies.append(remote(block, block, c_s.at[t, d], c_r.at[t, d], (i, 2 * along[d] + c)))
+            copies.append(remote(block, block, c_s.at[t], c_r.at[t], (i, 2 * along[d] + c)))
             copies[-1].start()
         return copies
 
@@ -241,13 +243,13 @@
         copies = []
         for d in (2, 1, 3):
             to = lax.rem(along[d] + 4, CHIPS)
-            copies.append(remote(block, block, d_s.at[t, d], d_r.at[t, d], (i, 2 * to + c)))
+            copies.append(remote(block, block, d_s.at[t], d_r.at[t], (i, 2 * to + c)))
             copies[-1].start()
         return copies
 
     def across(t):
         mine = nfull.at[PARTS[t][1], m, c, lines[PARTS[t][0]]]
-        return remote(mine, mine, z_s.at[t], z_r.at[t], (i, 2 * over + c))
+        return remote(mine, mine, d_s.at[t], d_r.at[t], (i, 2 * over + c))
 
     def to_other_core(t, first, n):
         part = nfull.at[PARTS[t][1], pl.ds(first, 4), c, lines[PARTS[t][0]]]
@@ -272,14 +274,11 @@
         proj_ref[lines[r], cols] = proj
 
     def near(t):
-        for copy in near_copies[t]:
-            got(copy)
+        got_all(nfull.at[PARTS[t][1], pl.ds(0, 3), c, lines[PARTS[t][0]]], c_s.at[t], c_r.at[t])
         to_other_core(t, 4 * z_hi, 0)
 
     def far(t):
-        got(across(t))
-        for copy in far_copies[t]:
-            got(copy)
+        got_all(nfull.at[PARTS[t][1], pl.ds(0, 4), c, lines[PARTS[t][0]]], d_s.at[t], d_r.at[t])
         to_other_core(t, 4 * (1 - z_hi), 1)
 
     def update(k):
@@ -353,20 +352,18 @@
             dma(R),
             dma(1),
             dma(1),
-            dma(R, CHIPS),
-            dma(R, CHIPS),
-            dma(R, CHIPS),
-            dma(R, CHIPS),
-            dma(n, CHIPS),
-            dma(n, CHIPS),
-            dma(n),
-            dma(n),
-            dma(n, 4),
-            dma(n, 4),
-            dma(n),
-            dma(n),
-            dma(n, 4),
-            dma(n, 4),
+            dma(R),
+            dma(R),
+            dma(R),
+            dma(R),
+            dma(n),
+            dma(n),
+            dma(n),
+            dma(n),
+            dma(n),
+            dma(n),
+            dma(n),
+            dma(n),
             dma(n, 2),
             dma(n, 2),
         ],

time: 49.4 us -> 47.9 us (0.970)
  Pallas kernels: 46.5 us -> 45 us
    pallas_call x1, Pallas kernels: 46.5 us -> 45 us  [shards(): pl.pallas_call(kernel, out_shape=(jax.ShapeDtypeStruct((DEEP, WIDE), bf16...]
where the time goes in v4:
time: 47.9 us; the launch traced here: 47.6 us
  Pallas kernels  45 us (94%)
  local copies, waits for them, and re-layouts  1.15 us (2%)
  other arithmetic  0.8 us (2%)
  between operations  0.67 us (1%)
    pallas_call x1, Pallas kernels, shards(): pl.pallas_call(kernel, out_shape=(jax.ShapeDtypeStruct((DEEP, WIDE), bf16...  45 us
    unnamed x5, local copies, waits for them, and re-layouts  1.15 us

profile of v4, /device:TPU:1, one launch (start us, length us, event | category | flops | bytes accessed | tf_op | source)
XLA Modules:
  0.0 47.6 jit_solution(13417070029093578065)
XLA Ops:
  0.6 0.0 copy-start.1
  0.6 0.0 copy-start
  0.7 45.0 %galore_step.1 = (bf16[512,1536]{1,0:T(8,128)(2,1)S(1)}, f32[32,1536]{1,0:T(8,128)S(1)}) custom-call(bf16[512,512]{1,0:T(8,128)(2,1)} %acts_ref.1, bf16[512,768]{1,0:T(8,128)(2,1)} %g_ref.1, bf16[512,512]{1,0:T(8,128)(2,1)} %basis_ref.1, f32[32,1536]{1,0:T(8,128)} %fm_ref.1, f32[32,1536]{1,0:T(8,128)} %sm_ref.1), custom_call_target="tpu_custom_call" | custom-call | flops 2000000000 | bytes 4194304 | tf_op jit(solution)/shard_map/galore_step/pallas_call | solution.py:325
  45.7 0.0 copy-done.1
  45.7 0.0 copy-done
  45.7 0.8 %fusion = (f32[32,1536]{1,0:T(8,128)}, f32[32,1536]{1,0:T(8,128)}) fusion(f32[32,1536]{1,0:T(8,128)S(1)} %get-tuple-element.6, f32[32,1536]{1,0:T(8,128)S(1)} %copy-done.1, f32[32,1536]{1,0:T(8,128)S(1)} %copy-done), kind=kLoop, calls=%fused_computation.1 | loop fusion | flops 344064 | bytes 983040 | tf_op jit(solution)/shard_map/add | solution.py:35
  46.5 1.1 %copy.9 = bf16[512,1536]{1,0:T(8,128)(2,1)} copy(bf16[512,1536]{1,0:T(8,128)(2,1)S(1)} %get-tuple-element.12) | data formatting | bytes 3145728
Async XLA Ops:
  0.6 45.1 %copy-start.1 = (f32[32,1536]{1,0:T(8,128)S(1)}, f32[32,1536]{1,0:T(8,128)}, u32[]{:S(2)}) copy-start(f32[32,1536]{1,0:T(8,128)} %sm_ref.1) | copy-start | bytes 589828
  0.6 45.1 %copy-start = (f32[32,1536]{1,0:T(8,128)S(1)}, f32[32,1536]{1,0:T(8,128)}, u32[]{:S(2)}) copy-start(f32[32,1536]{1,0:T(8,128)} %fm_ref.1) | copy-start | bytes 589828

commit v5 on v4

--- a/solution.py
+++ b/solution.py
@@ -24,11 +24,18 @@
 K = 2
 W = WIDE // K
 PARTS = [(r, k) for r in range(R) for k in range(K)]
-LAGS = {"reduce": 0.0, "moments": 3.9, "near": 6.9, "far": 9.3}
+STEPS = [
+    ("reduce", 0),
+    ("reduce", 1),
+    ("moments", 0),
+    ("reduce", 2),
+    ("reduce", 3),
+    ("moments", 1),
+    ("moments", 2),
+    ("moments", 3),
+] + [(name, t) for t in range(len(PARTS)) for name in ("near", "far")]
 FLUSH = {("reduce", 3), ("moments", 3), ("far", 3)}
 FAR_FIRST = [(0, 0), (1, 2), (1, 1), (1, 3), (0, 2), (1, 0), (0, 1), (0, 3)]
-GAP = 8.4 / len(PARTS)
-STEPS = sorted((lag + GAP * t, name, t) for name, lag in LAGS.items() for t in range(len(PARTS)))
 
 
 def new_moments(first, second, proj):
@@ -95,20 +102,20 @@
         pltpu.make_async_copy(fm_ref, fm, lsem.at[3]),
         pltpu.make_async_copy(sm_ref, sm, lsem.at[4]),
     ]
-    for load in loads:
+    for load in loads[:2]:
         load.start()
 
     barrier = pltpu.get_barrier_semaphore()
-    for d in range(1, CHIPS):
-        pl.semaphore_signal(barrier, inc=1, device_id=row_peers[d], device_id_type=MESH)
-        pl.semaphore_signal(barrier, inc=1, device_id=col_peers[d], device_id_type=MESH)
+    for to in (*row_peers[1:], pair, *col_peers[1:]):
+        pl.semaphore_signal(barrier, inc=1, device_id=to, device_id_type=MESH)
 
     @pl.when(jnp.logical_not(stays))
     def _():
         pl.semaphore_signal(barrier, inc=1, device_id=turned, device_id_type=MESH)
         pl.semaphore_signal(barrier, inc=1, device_id=comes, device_id_type=MESH)
 
-    pl.semaphore_signal(barrier, inc=1, device_id=pair, device_id_type=MESH)
+    for load in loads[2:]:
+        load.start()
 
     loads[0].wait()
     loads[1].wait()
@@ -296,7 +303,7 @@
 
     steps = {"reduce": reduce, "moments": moments, "near": near, "far": far}
     pending = []
-    for _, name, t in STEPS:
+    for name, t in STEPS:
         steps[name](t)
         if (name, t) in FLUSH:
             flush()

time: 47.9 us -> 47.6 us (level)
  no operation moved by 1% of the time
where the time goes in v5:
time: 47.6 us; the launch traced here: 47.4 us
  Pallas kernels  44.8 us (94%)
  local copies, waits for them, and re-layouts  1.15 us (2%)
  other arithmetic  0.8 us (2%)
  between operations  0.67 us (1%)
    pallas_call x1, Pallas kernels, shards(): pl.pallas_call(kernel, out_shape=(jax.ShapeDtypeStruct((DEEP, WIDE), bf16...  44.8 us
    unnamed x5, local copies, waits for them, and re-layouts  1.15 us

profile of v5, /device:TPU:1, one launch (start us, length us, event | category | flops | bytes accessed | tf_op | source)
XLA Modules:
  0.0 47.4 jit_solution(18336525189990332827)
XLA Ops:
  0.6 0.0 copy-start.1
  0.6 0.0 copy-start
  0.7 44.8 %galore_step.1 = (bf16[512,1536]{1,0:T(8,128)(2,1)S(1)}, f32[32,1536]{1,0:T(8,128)S(1)}) custom-call(bf16[512,512]{1,0:T(8,128)(2,1)} %acts_ref.1, bf16[512,768]{1,0:T(8,128)(2,1)} %g_ref.1, bf16[512,512]{1,0:T(8,128)(2,1)} %basis_ref.1, f32[32,1536]{1,0:T(8,128)} %fm_ref.1, f32[32,1536]{1,0:T(8,128)} %sm_ref.1), custom_call_target="tpu_custom_call" | custom-call | flops 2000000000 | bytes 4194304 | tf_op jit(solution)/shard_map/galore_step/pallas_call | solution.py:332
  45.5 0.0 copy-done.1
  45.5 0.0 copy-done
  45.5 0.8 %fusion = (f32[32,1536]{1,0:T(8,128)}, f32[32,1536]{1,0:T(8,128)}) fusion(f32[32,1536]{1,0:T(8,128)S(1)} %get-tuple-element.6, f32[32,1536]{1,0:T(8,128)S(1)} %copy-done.1, f32[32,1536]{1,0:T(8,128)S(1)} %copy-done), kind=kLoop, calls=%fused_computation.1 | loop fusion | flops 344064 | bytes 983040 | tf_op jit(solution)/shard_map/add | solution.py:42
  46.3 1.1 %copy.9 = bf16[512,1536]{1,0:T(8,128)(2,1)} copy(bf16[512,1536]{1,0:T(8,128)(2,1)S(1)} %get-tuple-element.12) | data formatting | bytes 3145728
Async XLA Ops:
  0.6 44.8 %copy-start.1 = (f32[32,1536]{1,0:T(8,128)S(1)}, f32[32,1536]{1,0:T(8,128)}, u32[]{:S(2)}) copy-start(f32[32,1536]{1,0:T(8,128)} %sm_ref.1) | copy-start | bytes 589828
  0.6 44.8 %copy-start = (f32[32,1536]{1,0:T(8,128)S(1)}, f32[32,1536]{1,0:T(8,128)}, u32[]{:S(2)}) copy-start(f32[32,1536]{1,0:T(8,128)} %fm_ref.1) | copy-start | bytes 589828
